TPU v7x, 512 devices: a whole 4x8x8 slice. The times are simulated.
512 devices in a mesh: cuts: 32 (over y, x_hi, core), mode: 16 (over x_lo, z).
Axes of the slice: x: 4 (x_hi: 2, x_lo: 2; x = x_hi * 2 + x_lo), y: 8, z: 8, core: 2. Of those that a mesh axis runs over, the one named last changes fastest.
Arguments:
- stem: float32 [32, 16, 16, 32768], P('cuts', 'mode'), may hold values from -1.5 to 1.5
- left: float32 [6, 2, 512, 512], P(None, None, 'mode'), may hold values from -0.25 to 0.25
- right: float32 [512, 512], replicated, may hold values from -0.25 to 0.25
- slice_bits: int32 [32, 6], P('cuts'), may hold values from 0 to 1
- leg_order: int32 [6, 9], replicated, may hold values from 0 to 8, each once within a row
Outputs:
- amplitudes: float32 [16, 16, 32768], P(None, 'mode', 'cuts')
Inputs may be any that keep to these rules, and one draw needn't show every extreme that they name: slice_bits[s, t] is the value of branch t's cut bond in slice s. Each row of leg_order is a permutation of 0 to 8.
All inputs are finite; a program needn't handle non-finite values.
Results may differ from a plain program's by a relative error of at most 0.00018.
Values sent between devices are 32-bit elements; how exact they have to be, the bound alone decides.
A program may use at most 64 MiB of HBM per device.

v0:
```python
import jax
import jax.numpy as jnp
from jax import lax
from jax.sharding import PartitionSpec as P

HIGHEST_PRECISION = lax.Precision.HIGHEST


def side_by_side(arrays, axis, dim, along):
    widths = [a.shape[along] for a in arrays]
    both = jnp.concatenate(arrays, axis=along)
    out = lax.all_gather(both, axis, axis=dim, tiled=True)
    return tuple(jnp.split(out, [sum(widths[:k]) for k in range(1, len(widths))], axis=along))


def in_blocks(shard, dim, size):
    before, after = (shard.shape[:dim], shard.shape[dim + 1 :])
    return jnp.moveaxis(shard.reshape(*before, size, -1, *after), dim, 0)


def summed_on_arrival(shard, axis, dim):
    tiles = in_blocks(shard, dim, lax.axis_size(axis))
    arrived = lax.all_to_all(tiles, axis, split_axis=0, concat_axis=0, tiled=True)
    return arrived.sum(axis=0)


def leg_columns(leg_map, leg_count):
    indices = jnp.arange(2**leg_count, dtype=jnp.int32)
    shifts = leg_count - 1 - leg_map
    chosen = jnp.right_shift(indices[:, None], shifts[None, :]) & 1
    powers = jnp.left_shift(
        jnp.ones((leg_count,), jnp.int32), leg_count - 1 - jnp.arange(leg_count, dtype=jnp.int32)
    )
    return jnp.sum(chosen * powers[None, :], axis=1)


def per_device(stem, left, right, slice_bits, leg_order):
    slices, leading, middle, trailing = stem.shape
    leg_count = leg_order.shape[1]
    branch_size = 2**leg_count
    total_modes = 8 + trailing.bit_length() - 1
    devices_mode = lax.axis_size("mode")
    picked = jnp.where((slice_bits == 1)[:, :, None, None], left[None, :, 1], left[None, :, 0])

    def branch_right(branch):
        return jnp.take(right, leg_columns(leg_order[branch], leg_count), axis=1)

    def build(fragment, permuted):
        count_a, count_b, width = fragment.shape
        product = jnp.dot(
            fragment.reshape(count_a * count_b, width), permuted, precision=HIGHEST_PRECISION
        )
        return product.reshape(count_a, count_b, branch_size)

    def group_rows(first):
        return side_by_side(
            (
                build(picked[:, first], branch_right(first)),
                build(picked[:, first + 1], branch_right(first + 1)),
                build(picked[:, first + 2], branch_right(first + 2)),
            ),
            "mode",
            1,
            0,
        )

    def fetch(branch, kernel, gathered):
        return kernel(gathered[branch % 3], 0)

    def run_absorb(tensor, first, branch, gathered):
        after = 2 ** (total_modes - first - leg_count)
        prefix = tensor.shape[1] // (branch_size * after)
        if after == 1:
            shaped = tensor.reshape(slices, prefix, branch_size)

            def kernel(fragment, offset):
                return jnp.einsum("sji,spi->spj", fragment, shaped, precision=HIGHEST_PRECISION)

        else:
            shaped = tensor.reshape(slices, prefix, branch_size, after)

            def kernel(fragment, offset):
                return jnp.einsum("sji,spir->spjr", fragment, shaped, precision=HIGHEST_PRECISION)

        return fetch(branch, kernel, gathered).reshape(slices, -1)

    tensor = stem.reshape(slices, -1)
    gathered = group_rows(0)
    tensor = run_absorb(tensor, total_modes - leg_count, 0, gathered)
    tensor = run_absorb(tensor, 6, 1, gathered)
    tensor = run_absorb(tensor, 4, 2, gathered)
    columns = middle // devices_mode
    head_states = leading * devices_mode
    inner_head = 2 ** (leg_count - 4)
    gathered = group_rows(3)
    head_matrix = gathered[0]
    head_blocks = head_matrix.reshape(slices, head_states, inner_head, head_states, inner_head)
    blocks = tensor.reshape(
        slices, leading, devices_mode, columns, inner_head, trailing // inner_head
    )
    received = lax.all_to_all(blocks, "mode", split_axis=2, concat_axis=1, tiled=True)
    arranged = received.reshape(slices, head_states, columns, inner_head, received.shape[5])
    result = jnp.einsum("sabcd,scxdr->saxbr", head_blocks, arranged, precision=HIGHEST_PRECISION)
    tensor = result.reshape(slices, -1)
    tensor = run_absorb(tensor, total_modes - leg_count, 4, gathered)
    inner_pair = 2 ** (leg_count - 2)
    shaped_pair = tensor.reshape(slices, 4, 4, columns, inner_pair, -1)

    def pair_kernel(fragment, offset):
        pieces = fragment.reshape(slices, fragment.shape[1], 4, inner_pair)
        return jnp.einsum("sjce,sacxer->sjaxr", pieces, shaped_pair, precision=HIGHEST_PRECISION)

    result = fetch(5, pair_kernel, gathered)
    result = result.reshape(slices, 4, inner_pair, 4, columns, -1).transpose(0, 3, 1, 4, 2, 5)
    tensor = result.reshape(slices, head_states, columns, trailing)
    summed = jnp.sum(tensor, axis=0)
    return summed_on_arrival(summed, "cuts", 2)


def solution(mesh):
    in_specs = (
        P("cuts", "mode", None, None),
        P(None, None, "mode", None),
        P(),
        P("cuts", None),
        P(),
    )
    out_specs = P(None, "mode", "cuts")
    return jax.shard_map(
        per_device, mesh=mesh, in_specs=in_specs, out_specs=out_specs, check_vma=False
    )
```

profile of v0, /device:TPU:1, one launch (start us, length us, event | category | flops | bytes accessed | tf_op | source)
XLA Modules:
  0.0 316.6 jit_solution(13849809581889204642)
XLA Ops:
  6.5 0.0 all-gather.5.cloned.1.call-start
  6.5 0.9 subtract_bitcast_fusion.5
  7.5 0.1 multiply_reduce_fusion.2
  7.6 0.5 compare_and_fusion.2
  8.1 0.6 compare_and_fusion
  8.7 1.2 compare_bitcast_fusion
  9.9 1.6 copy.47
  11.5 2.3 gather_fusion.5
  13.8 1.6 gather_fusion.4
  15.5 1.6 gather_fusion.3
  17.1 0.0 copy-start.2
  17.1 1.2 bitcast_select_fusion
  18.3 2.3 convolution_bitcast_fusion.2
  20.7 0.0 copy-done.2
  20.7 1.1 convolution_bitcast_fusion.3
  21.8 1.1 convolution_bitcast_fusion.4
  23.0 0.7 pad_maximum_fusion.1
  23.7 0.0 all-gather.5.cloned.1.call-update
  23.7 0.3 all-gather.3.cloned.1.call-start
  24.0 1.6 gather_fusion.2
  25.7 1.6 gather_fusion.1
  27.3 0.0 copy-start.1
  27.4 2.3 gather_fusion
  29.7 0.0 copy-start
  29.7 0.0 copy-done.1
  29.7 1.1 convolution_bitcast_fusion.5
  30.9 1.1 convolution_bitcast_fusion.6
  32.0 0.0 copy-done
  32.0 1.1 convolution_bitcast_fusion.7
  33.1 0.7 pad_maximum_fusion
  33.8 0.0 all-gather.3.cloned.1.call-update
  33.8 1.8 reshape.136
  35.6 63.1 %all-gather.5.cloned.1.call-done = f32[3,512,512]{2,1,0:T(8,128)} async-done(((f32[3,32,512]{2,1,0:T(8,128)}), f32[3,512,512]{2,1,0:T(8,128)}) %all-gather.5.cloned.1.call-update) | async-done | bytes 3145744 | tf_op jit(solution)/shard_map/all_gather | solution.py:12
  98.7 6.2 %convolution_bitcast_fusion.1 = f32[1024,512]{0,1:T(8,128)} fusion(f32[1024,512]{1,0:T(8,128)S(1)} %reshape.136, f32[3,512,512]{2,1,0:T(8,128)} %all-gather.5.cloned.1.call-done), kind=kOutput, calls=%fused_computation.14 | convolution fusion | flops 3221225472 | bytes 5242880 | tf_op jit(solution)/shard_map/sji,spi->spj/dot_general | solution.py:77
  104.9 1.9 copy.53
  106.8 2.1 reshape.137
  108.9 8.5 %convolution_bitcast_fusion = f32[1,4,512,256]{2,3,1,0:T(8,128)S(1)} fusion(f32[4,512,256]{2,1,0:T(8,128)} %reshape.137, f32[3,512,512]{2,1,0:T(8,128)} %all-gather.5.cloned.1.call-done), kind=kOutput, calls=%fused_computation.13 | convolution fusion | flops 3221225472 | bytes 5242880 | tf_op jit(solution)/shard_map/sji,spir->spjr/dot_general | solution.py:83
  117.4 1.9 copy.55
  119.3 1.8 reshape.139
  121.2 6.0 %fusion.14 = f32[1024,512]{0,1:T(8,128)} fusion(f32[512,1024]{1,0:T(8,128)S(1)} %reshape.139, f32[3,512,512]{2,1,0:T(8,128)} %all-gather.5.cloned.1.call-done), kind=kOutput, calls=%fused_computation.24 | convolution fusion | flops 3221225472 | bytes 5242880 | tf_op jit(solution)/shard_map/sji,spir->spjr/dot_general | solution.py:83
  127.2 4.6 %all-to-all-start = ((f32[1,1,16,1,32,1024]{5,4,3,1,0,2:T(8,128)}), f32[1,1,16,1,32,1024]{5,4,3,1,0,2:T(8,128)}, u32[]{:S(2)}, u32[]{:S(2)}) async-start(f32[1,1,16,1,32,1024]{5,4,3,1,0,2:T(8,128)} %bitcast.39), calls=%async_computation | async-start | bytes 4194304 | tf_op jit(solution)/shard_map/all_to_all | solution.py:101
  131.8 76.7 %all-gather.3.cloned.1.call-done = f32[3,512,512]{2,1,0:T(8,128)} async-done(((f32[3,32,512]{2,1,0:T(8,128)}), f32[3,512,512]{2,1,0:T(8,128)}) %all-gather.3.cloned.1.call-update) | async-done | bytes 3145744 | tf_op jit(solution)/shard_map/all_gather | solution.py:12
  208.6 1.7 fusion.46
  210.3 0.4 reshape.131
  210.7 2.5 reshape.142
  213.2 0.0 all-to-all-done
  213.2 10.6 %fusion.8 = f32[1,16,1,32,1024]{4,3,1,2,0:T(8,128)} fusion(f32[16,32,16,32]{3,2,1,0:T(8,128)} %reshape.142, f32[1,1,16,1,32,1024]{5,4,3,1,0,2:T(8,128)} %all-to-all-done), kind=kOutput, calls=%fused_computation.12 | convolution fusion | flops 3221225472 | bytes 5242880 | tf_op jit(solution)/shard_map/sabcd,scxdr->saxbr/dot_general | solution.py:103
  223.7 1.7 reshape.143
  225.5 6.0 %fusion.13 = f32[1024,512]{1,0:T(8,128)} fusion(f32[1024,512]{1,0:T(8,128)S(1)} %reshape.143, f32[3,512,512]{2,1,0:T(8,128)} %all-gather.3.cloned.1.call-done), kind=kOutput, calls=%fused_computation.22 | convolution fusion | flops 3221225472 | bytes 5242880 | tf_op jit(solution)/shard_map/sji,spi->spj/dot_general | solution.py:77
  231.5 2.7 reshape.145
  234.2 2.1 copy.58
  236.4 3.6 %fusion.5 = f32[1,4,4,1,128,256]{5,4,1,2,3,0:T(8,128)S(1)} fusion(f32[4,4,128,256]{2,3,1,0:T(8,128)S(1)} %copy.58, f32[4,128,4,128,1]{3,2,1,0,4:T(4,128)S(1)} %bitcast.142), kind=kOutput, calls=%fused_computation.11 | convolution fusion | flops 3221225472 | bytes 5242880 | tf_op jit(solution)/shard_map/sjce,sacxer->sjaxr/dot_general | solution.py:111
  239.9 0.1 copy.60
  240.1 1.7 reshape.146
  241.8 2.8 copy.61
  244.6 64.1 %all_to_all.14 = f32[32,16,1,1024]{3,1,2,0:T(8,128)S(1)} all-to-all(f32[32,16,1,1024]{3,1,2,0:T(8,128)S(1)} %copy.61), channel_id=1, replica_groups=mesh['cuts'=32,'mode'=16] {'cuts'}, dimensions={0} | all-to-all | bytes 4194304 | tf_op jit(solution)/shard_map/all_to_all | solution.py:23
  308.7 0.1 reduce_sum.75
  308.8 0.7 reduce_sum.76
  (11 shorter events, 0.1 us)
Async XLA Ops:
  6.5 92.2 %all-gather.5.cloned.1.call-start = ((), (), s32[]{:S(2)}) async-start(), calls=%async_computation.3 | async-start | bytes 3342336 | tf_op jit(solution)/shard_map/all_gather | solution.py:12
  17.1 3.6 %copy-start.2 = (pred[512]{0:T(512)(128)(4,1)S(1)}, pred[512]{0:T(512)(128)(4,1)}, u32[]{:S(2)}) copy-start(pred[512]{0:T(512)(128)(4,1)} %get-tuple-element.27) | copy-start | bytes 1540
  23.7 184.9 %all-gather.3.cloned.1.call-start = ((), (), s32[]{:S(2)}) async-start(), calls=%async_computation.2 | async-start | bytes 3342336 | tf_op jit(solution)/shard_map/all_gather | solution.py:12
  27.3 2.4 copy-start.1
  29.7 2.3 copy-start
  127.2 85.9 %all-to-all-start = ((f32[1,1,16,1,32,1024]{5,4,3,1,0,2:T(8,128)}), f32[1,1,16,1,32,1024]{5,4,3,1,0,2:T(8,128)}, u32[]{:S(2)}, u32[]{:S(2)}) async-start(f32[1,1,16,1,32,1024]{5,4,3,1,0,2:T(8,128)} %bitcast.39), calls=%async_computation | async-start | bytes 4194304 | tf_op jit(solution)/shard_map/all_to_all | solution.py:101
Sparse Core Ops, SparseCore 0:
  23.8 74.8 all-gather.4
  100.8 107.7 all-gather.2
where the time goes:
time: 321 us; the launch traced here: 317 us
  waiting for transfers between devices  140 us (44%)
  blocking collectives  64.1 us (20%)
  matrix products  48.9 us (15%)
  local copies, waits for them, and re-layouts  38.6 us (12%)
  between operations  13.9 us (4%)
  other arithmetic  6.15 us (2%)
  starting transfers between devices  4.94 us (2%)
    all_gather x2, waiting for transfers between devices, side_by_side(): out = lax.all_gather(both, axis, axis=dim, tiled=True)  140 us
    all_to_all x1, blocking collectives, summed_on_arrival(): lax.all_to_all(tiles, axis, split_axis=0, concat_axis=0, tiled=True)  64.1 us
    another operation x8, local copies, waits for them, and re-layouts  15.1 us
    dot_general x2, matrix products, kernel(): jnp.einsum('sji,spir->spjr', fragment, shaped, precision=HIGHEST_PRECISION)  14.6 us
    dot_general x2, matrix products, kernel(): jnp.einsum('sji,spi->spj', fragment, shaped, precision=HIGHEST_PRECISION)  12.2 us
    gather x6, local copies, waits for them, and re-layouts, branch_right(): return jnp.take(right, leg_columns(leg_order[branch], leg_count), axis=1)  11.2 us
    dot_general x1, matrix products, per_device(): jnp.einsum('sabcd,scxdr->saxbr', head_blocks, arranged, precision=HIGHEST...  10.6 us
    dot_general x6, matrix products, build(): jnp.dot(fragment.reshape(count_a * count_b, width), permuted, precision=H...  7.97 us
  transfers between devices with their start and end apart: 3, of which 2 were waited for; matrix products, arithmetic and copies ran while one was open for 14% of the time, Pallas kernels for 0%

commit v1 on v0

v1 whole, which is shorter than its diff:
```python
import functools

import jax
import jax.numpy as jnp
from jax import lax
from jax.experimental import pallas as pl
from jax.experimental.pallas import tpu as pltpu
from jax.sharding import PartitionSpec as P

F32, BF16, I32 = jnp.float32, jnp.bfloat16, jnp.int32
MESH = pl.DeviceIdType.MESH
LINE = (0, 2)
RING = (1, 4, 3, 5)
NATURAL9 = (0, 1, 2, 3, 4, 5, 6, 7, 8)
COLUMNS = {1: (8, 0, 1, 2, 3, 4, 5, 6, 7), 5: (7, 8, 0, 1, 2, 3, 4, 5, 6)}
ROWS = {1: (3, 4, 0, 1, 2), 5: (2, 1, 0, 3, 4)}


def halves(a):
    high = a.astype(BF16)
    return high, (a - high.astype(F32)).astype(BF16)


def dot(a, b, transposed=False):
    dims = (((1,), (1 if transposed else 0,)), ((), ()))
    return lax.dot_general(a, b, dims, preferred_element_type=F32)


def dot3(a, b, transposed=False):
    (ah, al), (bh, bl) = a, b
    return dot(ah, bl, transposed) + dot(al, bh, transposed) + dot(ah, bh, transposed)


def reordered(index, order):
    bits = len(order)
    total = jnp.zeros_like(index)
    for place, leg in enumerate(order):
        bit = jnp.right_shift(index, bits - 1 - place) & 1
        total = total + jnp.left_shift(bit, bits - 1 - leg)
    return total


def one_hot(rows, columns):
    return jnp.where(rows == columns, 1.0, 0.0).astype(BF16)


def fragments(order, bits, left, right, fz, fy, sel):
    product = dot3(halves(left[...].reshape(384, 512)), halves(right[...]))
    for t in range(6):
        part = product[64 * t : 64 * t + 64]
        first = part.astype(BF16)
        rest = part - first.astype(F32)
        second = rest.astype(BF16)
        third = (rest - second.astype(F32)).astype(BF16)
        stacked = jnp.concatenate([first, second, third], axis=0)
        spot = lax.broadcasted_iota(I32, (8, 512), 1)
        spot = reordered(spot, COLUMNS.get(t, NATURAL9))
        column = jnp.zeros_like(spot)
        for q in range(9):
            bit = jnp.right_shift(spot, jnp.full_like(spot, 8 - order[t, q])) & 1
            column = column + jnp.left_shift(bit, 8 - q)
        moved = dot(stacked, one_hot(lax.broadcasted_iota(I32, (512, 512), 0), column[0:1]))
        pieces = [moved[64 * k : 64 * k + 64] for k in range(3)]
        if t in ROWS:
            new = lax.broadcasted_iota(I32, (64, 64), 0)
            old = (new & 32) + reordered(new & 31, ROWS[t])
            turn = one_hot(lax.broadcasted_iota(I32, (64, 64), 1), old)
            pieces = [dot(turn, p.astype(BF16)) for p in pieces]
        value = pieces[0] + pieces[1] + pieces[2]
        mine = jnp.full((8, 256), bits[0, t], I32)
        if t in LINE:
            wide = jnp.full((32, 512), bits[0, t], I32)
            fz[LINE.index(t)] = jnp.where(wide == 1, value[32:], value[:32])
        else:
            k = RING.index(t)
            sel[k] = mine
            for s in range(8):
                for h in range(2):
                    fy[k, s, h] = value[8 * s : 8 * s + 8, 256 * h : 256 * h + 256]


def contract(
    stem, fz, fy, sel, out,
    gz, gy, bh, bl, y0, y1, w, tt, rr, s3, acc, twin, part, final, last,
    z_send, z_recv, x_send, x_recv, base_send, base_recv, y_send, y_recv, d_send, d_recv,
    a_send, a_recv, t_send, t_recv, r_send, r_recv, l_send, l_recv,
):
    c, m = lax.axis_index("cuts"), lax.axis_index("mode")
    xl, z = m // 8, lax.rem(m, 8)
    y, xh, core = c // 4, lax.rem(c // 2, 2), lax.rem(c, 2)
    z_next = [(c, xl * 8 + lax.rem(z + 1, 8)), (c, xl * 8 + lax.rem(z + 7, 8))]
    y_next = [(lax.rem(y + 1, 8) * 4 + lax.rem(c, 4), m), (lax.rem(y + 7, 8) * 4 + lax.rem(c, 4), m)]
    sibling = (c + 1 - 2 * core, m)
    across = (c + 2 - 4 * xh, m)
    beside = (c, m + 8 - 16 * xl)

    def peer(k):
        return lax.rem(m + k, 16)

    barrier = pltpu.get_barrier_semaphore()

    @pl.loop(1, 16)
    def _(k):
        pl.semaphore_signal(barrier, inc=1, device_id=(c, peer(k)), device_id_type=MESH)

    for target in (*y_next, sibling, across):
        pl.semaphore_signal(barrier, inc=1, device_id=target, device_id_type=MESH)
    for k in range(2):
        gz[k, m] = fz[k]
    for t in range(4):
        gy[t, y, core, m] = fy[t, y, core]
    pl.semaphore_wait(barrier, 19)

    started = []

    def remote(src, dst, send, recv, target):
        return pltpu.make_async_remote_copy(
            src_ref=src, dst_ref=dst, send_sem=send, recv_sem=recv, device_id=target, device_id_type=MESH
        )

    def go(copy):
        copy.start()
        started.append(copy)

    def x_copy(k):
        return remote(gz.at[k, m], gz.at[k, m], x_send.at[k], x_recv.at[k], beside)

    def z_copy(k, cls, d, s):
        owner = lax.rem(z + 8 - (1 - 2 * d) * (s - 1), 8)
        row = (xl * 8 if cls == 0 else (1 - xl) * 8) + owner
        piece = gz.at[k, row]
        if s == 4:
            piece = gz.at[k, row, pl.ds(16 * d, 16)]
        return remote(piece, piece, z_send.at[k, cls, d, s - 1], z_recv.at[k, cls, d, s - 1], z_next[d])

    def z_step(k, s):
        for cls in range(2):
            if s == 1 and cls == 1:
                x_copy(k).wait_recv()
            for d in range(2):
                if s > 1:
                    z_copy(k, cls, d, s - 1).wait_recv()
                go(z_copy(k, cls, d, s))

    def z_finish(k):
        for cls in range(2):
            for d in range(2):
                z_copy(k, cls, d, 4).wait_recv()

    def base_copy(g, k):
        pair = pl.ds(2 * g, 2)
        return remote(
            fy.at[pair, y, core], gy.at[pair, y, core, m],
            base_send.at[g, k], base_recv.at[g, k], (c, peer(k)),
        )

    def base_start(g):
        @pl.loop(1, 16)
        def _(k):
            base_copy(g, k).start()

    def base_wait(g):
        @pl.loop(1, 16)
        def _(k):
            base_copy(g, k).wait_recv()

    def y_copy(t, d, s):
        owner = lax.rem(y + 8 - (1 - 2 * d) * (s - 1), 8)
        piece = gy.at[t, owner, core]
        if s == 4:
            piece = gy.at[t, owner, core, pl.ds(8 * d, 8)]
        return remote(piece, piece, y_send.at[t, d, s - 1], y_recv.at[t, d, s - 1], y_next[d])

    def d_copy(t, n):
        if n == 0:
            slot = y
        elif n == 7:
            slot = lax.rem(y + 4, 8)
        else:
            slot = lax.rem(y + 8 - (1 - 2 * ((n - 1) % 2)) * ((n + 1) // 2), 8)
        piece = gy.at[t, slot, core]
        return remote(piece, piece, d_send.at[t, n], d_recv.at[t, n], sibling)

    def y_step(t, s):
        if s == 1:
            if t % 2 == 0:
                base_wait(t // 2)
            for d in range(2):
                go(y_copy(t, d, 1))
            go(d_copy(t, 0))
            return
        for d in range(2):
            y_copy(t, d, s - 1).wait_recv()
            if s < 5:
                go(y_copy(t, d, s))
                go(d_copy(t, 2 * (s - 1) - 1 + d))
        if s == 5:
            go(d_copy(t, 7))

    def y_finish(t):
        for n in range(8):
            d_copy(t, n).wait_recv()

    def prepare_line(k):
        b = LINE[k]

        @pl.loop(0, 4)
        def _(i):
            rows = pl.ds(pl.multiple_of(128 * i, 128), 128)
            bh[b, rows], bl[b, rows] = halves(gz[k, pl.ds(4 * i, 4)].reshape(128, 512))

    def prepare_ring(t):
        b = RING[t]
        one = sel[t] == 1

        @pl.loop(0, 16)
        def _(i):
            rows = pl.ds(pl.multiple_of(32 * i, 32), 32)
            for h in range(2):
                lanes = slice(256 * h, 256 * h + 256)
                value = jnp.concatenate(
                    [jnp.where(one, gy[t, 4 + q, h, i], gy[t, q, h, i]) for q in range(4)], axis=0
                )
                bh[b, rows, lanes], bl[b, rows, lanes] = halves(value)

    def prepare_turned(t, turn=None):
        b = RING[t]
        one = (sel[t] == 1)[None]

        @pl.loop(0, 4)
        def _(q):
            rows = pl.ds(pl.multiple_of(128 * q, 128), 128)
            for h in range(2):
                lanes = slice(256 * h, 256 * h + 256)
                value = jnp.where(one, gy[t, 4 + q, h], gy[t, q, h]).reshape(128, 256)
                high, low = halves(value)
                if turn is not None:
                    high, low = dot(turn, high).astype(BF16), dot(turn, low).astype(BF16)
                bh[b, rows, lanes], bl[b, rows, lanes] = high, low

    def matrix(b):
        return bh[b], bl[b]

    def absorb0():
        @pl.loop(0, 2)
        def _(i):
            rows = pl.ds(pl.multiple_of(512 * i, 512), 512)
            y0[rows] = dot3(halves(stem[rows]), matrix(0), True)

    def absorb1():
        @pl.loop(0, 4)
        def _(i):
            rows = pl.ds(pl.multiple_of(256 * i, 256), 256)
            data = jnp.concatenate([y0[rows, :256], y0[rows, 256:]], axis=0)
            new = dot3(matrix(1), halves(data))
            for m13 in range(2):
                for h in range(2):
                    at = 128 * (2 * m13 + h)
                    y1[h, i, m13] = new[at : at + 128]

    def absorb4():
        @pl.loop(0, 2)
        def _(i):
            pair = pl.ds(2 * i, 2)
            data = jnp.concatenate([y1[0, pair].reshape(512, 256), y1[1, pair].reshape(512, 256)], axis=1)
            new = dot3(halves(data), matrix(4), True)
            for k in range(2):
                for m13 in range(2):
                    for h in range(2):
                        at = 128 * (2 * k + m13)
                        w[2 * m13 + h, 2 * i + k] = new[at : at + 128, 256 * h : 256 * h + 256]

    def a_copy(q, k):
        return remote(
            tt.at[q, peer(k)], rr.at[q, m], a_send.at[q, k], a_recv.at[q, k], (c, peer(k))
        )

    def absorb2():
        @pl.loop(0, 4)
        def _(q):
            new = dot3(matrix(2), halves(w[q].reshape(512, 256)))
            tt[q] = new.reshape(16, 32, 256)
            rr[q, m] = tt[q, m]

            @pl.loop(1, 16)
            def _(k):
                a_copy(q, k).start()

    def absorb3():
        @pl.loop(0, 4)
        def _(q):
            @pl.loop(1, 16)
            def _(k):
                a_copy(q, k).wait_recv()

            new = dot3(matrix(3), halves(rr[q].reshape(512, 256)))
            s3[q] = new.reshape(4, 128, 256)

    def t_copy(i):
        return remote(acc.at[1 - core, i], twin.at[i], t_send.at[i], t_recv.at[i], sibling)

    def absorb5(half, send):
        rows = pl.ds(pl.multiple_of(256 * half, 256), 256)

        @pl.loop(0, 4)
        def _(i):
            data = s3[:, i].reshape(512, 256)
            new = dot3((bh[5, rows], bl[5, rows]), halves(data)).reshape(2, 8, 16, 256)
            if send:
                acc[half, i] = new
                t_copy(i).start()
            else:
                t_copy(i).wait_recv()
                acc[half, i] = new + twin[i]

    def steps(k, d):
        return 4 if k == d else 3

    def r_copy(k, d, s):
        n = steps(k, d)
        dest = lax.rem(y + 8 + (1 - 2 * d) * (n - s + 1), 8)
        src = acc.at[core, :, k, dest] if s == 1 else part.at[k, d, s - 2]
        return remote(src, part.at[k, d, s - 1], r_send.at[k, d, s - 1], r_recv.at[k, d, s - 1], y_next[d])

    def reduce():
        order = [(k, d) for d in range(2) for k in range(2)]
        for k, d in order:
            go(r_copy(k, d, 1))
        for s in range(2, 5):
            for k, d in order:
                n = steps(k, d)
                if s <= n:
                    dest = lax.rem(y + 8 + (1 - 2 * d) * (n - s + 1), 8)
                    r_copy(k, d, s - 1).wait_recv()
                    part[k, d, s - 2] = part[k, d, s - 2] + acc[core, :, k, dest]
                    go(r_copy(k, d, s))
        for k in range(2):
            for d in range(2):
                r_copy(k, d, steps(k, d)).wait_recv()
            final[k] = acc[core, :, k, y] + part[k, 0, steps(k, 0) - 1] + part[k, 1, steps(k, 1) - 1]
        swap = remote(final.at[1 - xh], last, l_send, l_recv, across)
        go(swap)
        swap.wait_recv()
        out[...] = (final[xh] + last[...]).reshape(64, 256)

    go(x_copy(0))
    base_start(0)
    z_step(0, 1)
    z_step(0, 2)
    y_step(0, 1)
    go(x_copy(1))
    z_step(1, 1)
    z_step(0, 3)
    y_step(0, 2)
    y_step(1, 1)
    base_start(1)
    z_step(1, 2)
    z_step(0, 4)
    y_step(0, 3)
    y_step(1, 2)
    z_step(1, 3)
    z_finish(0)
    y_step(0, 4)
    y_step(1, 3)
    z_step(1, 4)
    prepare_line(0)
    absorb0()
    y_step(0, 5)
    y_step(1, 4)
    y_step(2, 1)
    y_finish(0)
    prepare_turned(0)
    absorb1()
    y_step(1, 5)
    y_step(2, 2)
    y_step(3, 1)
    y_finish(1)
    prepare_ring(1)
    absorb4()
    y_step(2, 3)
    y_step(3, 2)
    z_finish(1)
    prepare_line(1)
    absorb2()
    y_step(2, 4)
    y_step(3, 3)
    y_step(2, 5)
    y_finish(2)
    prepare_ring(2)
    y_step(3, 4)
    y_step(3, 5)
    y_finish(3)
    new = lax.broadcasted_iota(I32, (128, 128), 0)
    old = reordered(new, (2, 3, 4, 0, 1, 5, 6))
    prepare_turned(3, one_hot(lax.broadcasted_iota(I32, (128, 128), 1), old))
    absorb3()
    absorb5(1 - core, True)
    absorb5(core, False)
    reduce()

    for copy in started:
        copy.wait_send()

    @pl.loop(1, 16)
    def _(k):
        for g in range(2):
            base_copy(g, k).wait_send()

    @pl.loop(0, 4)
    def _(q):
        t_copy(q).wait_send()

        @pl.loop(1, 16)
        def _(k):
            a_copy(q, k).wait_send()


def per_device(stem, left, right, slice_bits, leg_order):
    smem, vmem = pl.BlockSpec(memory_space=pltpu.SMEM), pl.BlockSpec(memory_space=pltpu.VMEM)
    shape = jax.ShapeDtypeStruct
    fz, fy, sel = pl.pallas_call(
        fragments,
        out_shape=(shape((2, 32, 512), F32), shape((4, 8, 2, 8, 256), F32), shape((4, 8, 256), I32)),
        in_specs=[smem, smem, vmem, vmem],
        out_specs=(vmem, vmem, vmem),
        compiler_params=pltpu.CompilerParams(vmem_limit_bytes=32 * 2**20),
    )(leg_order, slice_bits, left, right)
    dma = pltpu.SemaphoreType.DMA
    result = pl.pallas_call(
        contract,
        out_shape=shape((64, 256), F32),
        in_specs=[vmem, vmem, vmem, vmem],
        out_specs=vmem,
        scratch_shapes=[
            pltpu.VMEM((2, 16, 32, 512), F32),
            pltpu.VMEM((4, 8, 2, 16, 8, 256), F32),
            pltpu.VMEM((6, 512, 512), BF16),
            pltpu.VMEM((6, 512, 512), BF16),
            pltpu.VMEM((1024, 512), F32),
            pltpu.VMEM((2, 4, 2, 128, 256), F32),
            pltpu.VMEM((4, 4, 128, 256), F32),
            pltpu.VMEM((4, 16, 32, 256), F32),
            pltpu.VMEM((4, 16, 32, 256), F32),
            pltpu.VMEM((4, 4, 128, 256), F32),
            pltpu.VMEM((2, 4, 2, 8, 16, 256), F32),
            pltpu.VMEM((4, 2, 8, 16, 256), F32),
            pltpu.VMEM((2, 2, 4, 4, 16, 256), F32),
            pltpu.VMEM((2, 4, 16, 256), F32),
            pltpu.VMEM((4, 16, 256), F32),
            dma((2, 2, 2, 4)), dma((2, 2, 2, 4)), dma((2,)), dma((2,)),
            dma((2, 16)), dma((2, 16)), dma((4, 2, 4)), dma((4, 2, 4)), dma((4, 8)), dma((4, 8)),
            dma((4, 16)), dma((4, 16)), dma((4,)), dma((4,)), dma((2, 2, 4)), dma((2, 2, 4)), dma, dma,
        ],
        compiler_params=pltpu.CompilerParams(
            collective_id=0, has_side_effects=True, vmem_limit_bytes=56 * 2**20
        ),
    )(stem.reshape(1024, 512), fz, fy, sel)
    return result.reshape(16, 1, 1024)


def solution(mesh):
    in_specs = (
        P("cuts", "mode", None, None),
        P(None, None, "mode", None),
        P(),
        P("cuts", None),
        P(),
    )
    out_specs = P(None, "mode", "cuts")
    return jax.shard_map(per_device, mesh=mesh, in_specs=in_specs, out_specs=out_specs, check_vma=False)
```

time: 321 us -> 155 us (0.48)
  the two profiles are of different devices: /device:TPU:1 before, /device:TPU:8 now
where the time goes in v1:
time: 155 us
  Pallas kernels  144 us (93%)
  local copies, waits for them, and re-layouts  10.1 us (7%)
    pallas_call x1, Pallas kernels, per_device(): pl.pallas_call(contract, out_shape=shape((64, 256), F32), in_specs=[vmem,...  142 us
    unnamed x14, local copies, waits for them, and re-layouts  5.76 us

profile of v1, /device:TPU:8, one launch (start us, length us, event | category | flops | bytes accessed | tf_op | source)
XLA Modules:
  0.0 154.5 jit_solution(17636979500498730683)
XLA Ops:
  0.0 0.0 copy-start
  0.0 1.2 copy-done
  1.2 0.0 copy-start.1
  1.2 1.1 copy-done.1
  2.4 0.0 copy-start.5
  2.4 0.7 copy-done.5
  3.0 0.0 copy-start.6
  3.0 0.7 copy-done.6
  3.7 2.7 %shard_map.55 = (f32[2,32,512]{2,1,0:T(8,128)S(1)}, f32[4,8,2,8,256]{4,3,2,1,0:T(8,128)S(1)}, s32[4,8,256]{2,1,0:T(8,128)S(1)}) custom-call(s32[6,9]{1,0:T(8,128)S(1)} %copy-done.5, s32[1,6]{1,0:T(1,128)S(1)} %copy-done.6, f32[6,2,32,512]{3,2,1,0:T(8,128)S(1)} %copy-done.1, f32[512,512]{1,0:T(8,128)S(1)} %copy-done), custom_call_target="tpu_custom_call" | custom-call | tf_op jit(solution)/shard_map/pallas_call | solution.py:421
  6.4 0.0 copy-start.2
  6.4 0.8 copy-done.2
  7.2 0.0 copy-start.3
  7.2 0.7 copy-done.3
  7.8 0.0 copy-start.4
  7.8 0.6 copy-done.4
  8.5 2.8 %reshape.6.stem = f32[1024,512]{1,0:T(8,128)} reshape(f32[1,1,16,32768]{3,2,1,0:T(8,128)} %param.5) | data formatting | bytes 4194304 | tf_op jit(solution)/shard_map/reshape | solution.py:457
  11.2 141.8 %shard_map.56 = f32[64,256]{1,0:T(8,128)} custom-call(f32[1024,512]{1,0:T(8,128)} %reshape.6.stem, f32[2,32,512]{2,1,0:T(8,128)} %copy-done.3, f32[4,8,2,8,256]{4,3,2,1,0:T(8,128)} %copy-done.2, s32[4,8,256]{2,1,0:T(8,128)} %copy-done.4), custom_call_target="tpu_custom_call" | custom-call | tf_op jit(solution)/shard_map/pallas_call | solution.py:429
  153.0 1.5 reshape.8
Async XLA Ops:
  0.0 1.2 copy-start
  1.2 1.1 copy-start.1
  2.4 0.7 copy-start.5
  3.0 0.7 copy-start.6
  6.4 0.8 copy-start.2
  7.2 0.7 copy-start.3
  7.8 0.6 copy-start.4

commit v2 on v1

--- a/solution.py
+++ b/solution.py
@@ -10,9 +10,9 @@
 F32, BF16, I32 = jnp.float32, jnp.bfloat16, jnp.int32
 MESH = pl.DeviceIdType.MESH
 LINE = (0, 2)
-RING = (1, 4, 3, 5)
+RING = (1, 3, 4, 5)
 NATURAL9 = (0, 1, 2, 3, 4, 5, 6, 7, 8)
-COLUMNS = {1: (8, 0, 1, 2, 3, 4, 5, 6, 7), 5: (7, 8, 0, 1, 2, 3, 4, 5, 6)}
+COLUMNS = {1: (8, 2, 3, 4, 5, 6, 7, 0, 1), 5: (7, 8, 0, 1, 2, 3, 4, 5, 6)}
 ROWS = {1: (3, 4, 0, 1, 2), 5: (2, 1, 0, 3, 4)}
 
 
@@ -44,12 +44,60 @@
     return jnp.where(rows == columns, 1.0, 0.0).astype(BF16)
 
 
-def fragments(order, bits, left, right, fz, fy, sel):
-    product = dot3(halves(left[...].reshape(384, 512)), halves(right[...]))
-    for t in range(6):
-        part = product[64 * t : 64 * t + 64]
-        first = part.astype(BF16)
-        rest = part - first.astype(F32)
+def contract(
+    order, bits, stem_hbm, left_hbm, right_hbm, out,
+    left, right, stem, product, fy, xh, xl_, gz, gy, bh, bl, y0, w, tt, rr, s3, acc, twin, part, final, last,
+    in_sem, z_send, z_recv, x_send, x_recv, base_send, base_recv, y_send, y_recv, d_send, d_recv,
+    a_send, a_recv, t_send, t_recv, r_send, r_recv, l_send, l_recv,
+):
+    c, m = lax.axis_index("cuts"), lax.axis_index("mode")
+    xl, z = m // 8, lax.rem(m, 8)
+    y, xh_, core = c // 4, lax.rem(c // 2, 2), lax.rem(c, 2)
+    z_next = [(c, xl * 8 + lax.rem(z + 1, 8)), (c, xl * 8 + lax.rem(z + 7, 8))]
+    y_next = [(lax.rem(y + 1, 8) * 4 + lax.rem(c, 4), m), (lax.rem(y + 7, 8) * 4 + lax.rem(c, 4), m)]
+    sibling = (c + 1 - 2 * core, m)
+    across = (c + 2 - 4 * xh_, m)
+    beside = (c, m + 8 - 16 * xl)
+
+    def peer(k):
+        return lax.rem(m + k, 16)
+
+    barrier = pltpu.get_barrier_semaphore()
+
+    @pl.loop(1, 16)
+    def _(k):
+        pl.semaphore_signal(barrier, inc=1, device_id=(c, peer(k)), device_id_type=MESH)
+
+    for target in (*y_next, sibling, across):
+        pl.semaphore_signal(barrier, inc=1, device_id=target, device_id_type=MESH)
+
+    loads = [
+        pltpu.make_async_copy(src, dst, in_sem.at[n])
+        for n, (src, dst) in enumerate(((right_hbm, right), (left_hbm, left), (stem_hbm, stem)))
+    ]
+    for load in loads:
+        load.start()
+
+    started = []
+
+    def remote(src, dst, send, recv, target):
+        return pltpu.make_async_remote_copy(
+            src_ref=src, dst_ref=dst, send_sem=send, recv_sem=recv, device_id=target, device_id_type=MESH
+        )
+
+    def go(copy):
+        copy.start()
+        started.append(copy)
+
+    def multiply():
+        loads[0].wait()
+        loads[1].wait()
+        product[...] = dot3(halves(left[...].reshape(384, 512)), halves(right[...]))
+
+    def fragment(t):
+        value = product[64 * t : 64 * t + 64]
+        first = value.astype(BF16)
+        rest = value - first.astype(F32)
         second = rest.astype(BF16)
         third = (rest - second.astype(F32)).astype(BF16)
         stacked = jnp.concatenate([first, second, third], axis=0)
@@ -67,63 +115,39 @@
             turn = one_hot(lax.broadcasted_iota(I32, (64, 64), 1), old)
             pieces = [dot(turn, p.astype(BF16)) for p in pieces]
         value = pieces[0] + pieces[1] + pieces[2]
-        mine = jnp.full((8, 256), bits[0, t], I32)
         if t in LINE:
             wide = jnp.full((32, 512), bits[0, t], I32)
-            fz[LINE.index(t)] = jnp.where(wide == 1, value[32:], value[:32])
+            gz[LINE.index(t), m] = jnp.where(wide == 1, value[32:], value[:32])
         else:
             k = RING.index(t)
-            sel[k] = mine
             for s in range(8):
                 for h in range(2):
                     fy[k, s, h] = value[8 * s : 8 * s + 8, 256 * h : 256 * h + 256]
-
-
-def contract(
-    stem, fz, fy, sel, out,
-    gz, gy, bh, bl, y0, y1, w, tt, rr, s3, acc, twin, part, final, last,
-    z_send, z_recv, x_send, x_recv, base_send, base_recv, y_send, y_recv, d_send, d_recv,
-    a_send, a_recv, t_send, t_recv, r_send, r_recv, l_send, l_recv,
-):
-    c, m = lax.axis_index("cuts"), lax.axis_index("mode")
-    xl, z = m // 8, lax.rem(m, 8)
-    y, xh, core = c // 4, lax.rem(c // 2, 2), lax.rem(c, 2)
-    z_next = [(c, xl * 8 + lax.rem(z + 1, 8)), (c, xl * 8 + lax.rem(z + 7, 8))]
-    y_next = [(lax.rem(y + 1, 8) * 4 + lax.rem(c, 4), m), (lax.rem(y + 7, 8) * 4 + lax.rem(c, 4), m)]
-    sibling = (c + 1 - 2 * core, m)
-    across = (c + 2 - 4 * xh, m)
-    beside = (c, m + 8 - 16 * xl)
-
-    def peer(k):
-        return lax.rem(m + k, 16)
-
-    barrier = pltpu.get_barrier_semaphore()
-
-    @pl.loop(1, 16)
-    def _(k):
-        pl.semaphore_signal(barrier, inc=1, device_id=(c, peer(k)), device_id_type=MESH)
-
-    for target in (*y_next, sibling, across):
-        pl.semaphore_signal(barrier, inc=1, device_id=target, device_id_type=MESH)
-    for k in range(2):
-        gz[k, m] = fz[k]
-    for t in range(4):
-        gy[t, y, core, m] = fy[t, y, core]
-    pl.semaphore_wait(barrier, 19)
-
-    started = []
-
-    def remote(src, dst, send, recv, target):
-        return pltpu.make_async_remote_copy(
-            src_ref=src, dst_ref=dst, send_sem=send, recv_sem=recv, device_id=target, device_id_type=MESH
-        )
-
-    def go(copy):
-        copy.start()
-        started.append(copy)
-
-    def x_copy(k):
-        return remote(gz.at[k, m], gz.at[k, m], x_send.at[k], x_recv.at[k], beside)
+            gy[k, y, core, m] = fy[k, y, core]
+
+    def split_stem():
+        loads[2].wait()
+        upper = lax.broadcasted_iota(I32, (8, 512), 0) < 4
+
+        @pl.loop(0, 16)
+        def _(i):
+            for m4 in range(2):
+                a = [stem[8 * m4 : 8 * m4 + 8, pl.ds(pl.multiple_of(2048 * i, 2048) + 512 * j, 512)] for j in range(4)]
+                low = [jnp.where(upper, a[j], pltpu.roll(a[j + 1], 4, 0)) for j in (0, 2)]
+                high = [jnp.where(upper, pltpu.roll(a[j], 4, 0), a[j + 1]) for j in (0, 2)]
+                for m5, tiles in enumerate((low, high)):
+                    rows = pl.ds(pl.multiple_of(256 * (2 * m4 + m5) + 16 * i, 16), 16)
+                    xh[rows], xl_[rows] = halves(jnp.concatenate(tiles, axis=0))
+
+    def x_copy(k, n):
+        if n == 0:
+            owner = z
+        elif n == 7:
+            owner = lax.rem(z + 4, 8)
+        else:
+            owner = lax.rem(z + 8 - (1 - 2 * ((n - 1) % 2)) * ((n + 1) // 2), 8)
+        piece = gz.at[k, xl * 8 + owner]
+        return remote(piece, piece, x_send.at[k, n], x_recv.at[k, n], beside)
 
     def z_copy(k, cls, d, s):
         owner = lax.rem(z + 8 - (1 - 2 * d) * (s - 1), 8)
@@ -133,19 +157,33 @@
             piece = gz.at[k, row, pl.ds(16 * d, 16)]
         return remote(piece, piece, z_send.at[k, cls, d, s - 1], z_recv.at[k, cls, d, s - 1], z_next[d])
 
+    def z_first(k):
+        go(x_copy(k, 0))
+        for d in range(2):
+            go(z_copy(k, 0, d, 1))
+
+    def z_other(k):
+        x_copy(k, 0).wait_recv()
+        for d in range(2):
+            go(z_copy(k, 1, d, 1))
+
     def z_step(k, s):
-        for cls in range(2):
-            if s == 1 and cls == 1:
-                x_copy(k).wait_recv()
+        for cls in range(2 if k == 0 else 1):
             for d in range(2):
-                if s > 1:
-                    z_copy(k, cls, d, s - 1).wait_recv()
-                go(z_copy(k, cls, d, s))
+                z_copy(k, cls, d, s - 1).wait_recv()
+                if s < 5:
+                    go(z_copy(k, cls, d, s))
+                    if k == 1:
+                        go(x_copy(k, 2 * (s - 1) - 1 + d))
+        if k == 1 and s == 5:
+            go(x_copy(k, 7))
 
     def z_finish(k):
-        for cls in range(2):
-            for d in range(2):
-                z_copy(k, cls, d, 4).wait_recv()
+        if k == 0:
+            z_step(0, 5)
+        else:
+            for n in range(8):
+                x_copy(k, n).wait_recv()
 
     def base_copy(g, k):
         pair = pl.ds(2 * g, 2)
@@ -211,7 +249,7 @@
 
     def prepare_ring(t):
         b = RING[t]
-        one = sel[t] == 1
+        one = jnp.full((8, 256), bits[0, b], I32) == 1
 
         @pl.loop(0, 16)
         def _(i):
@@ -225,7 +263,7 @@
 
     def prepare_turned(t, turn=None):
         b = RING[t]
-        one = (sel[t] == 1)[None]
+        one = jnp.full((1, 8, 256), bits[0, b], I32) == 1
 
         @pl.loop(0, 4)
         def _(q):
@@ -245,30 +283,14 @@
         @pl.loop(0, 2)
         def _(i):
             rows = pl.ds(pl.multiple_of(512 * i, 512), 512)
-            y0[rows] = dot3(halves(stem[rows]), matrix(0), True)
+            y0[rows] = dot3((xh[rows], xl_[rows]), matrix(0), True)
 
     def absorb1():
         @pl.loop(0, 4)
         def _(i):
             rows = pl.ds(pl.multiple_of(256 * i, 256), 256)
             data = jnp.concatenate([y0[rows, :256], y0[rows, 256:]], axis=0)
-            new = dot3(matrix(1), halves(data))
-            for m13 in range(2):
-                for h in range(2):
-                    at = 128 * (2 * m13 + h)
-                    y1[h, i, m13] = new[at : at + 128]
-
-    def absorb4():
-        @pl.loop(0, 2)
-        def _(i):
-            pair = pl.ds(2 * i, 2)
-            data = jnp.concatenate([y1[0, pair].reshape(512, 256), y1[1, pair].reshape(512, 256)], axis=1)
-            new = dot3(halves(data), matrix(4), True)
-            for k in range(2):
-                for m13 in range(2):
-                    for h in range(2):
-                        at = 128 * (2 * k + m13)
-                        w[2 * m13 + h, 2 * i + k] = new[at : at + 128, 256 * h : 256 * h + 256]
+            w[:, i] = dot3(matrix(1), halves(data)).reshape(4, 128, 256)
 
     def a_copy(q, k):
         return remote(
@@ -286,15 +308,23 @@
             def _(k):
                 a_copy(q, k).start()
 
-    def absorb3():
-        @pl.loop(0, 4)
-        def _(q):
-            @pl.loop(1, 16)
-            def _(k):
-                a_copy(q, k).wait_recv()
-
-            new = dot3(matrix(3), halves(rr[q].reshape(512, 256)))
-            s3[q] = new.reshape(4, 128, 256)
+    def absorb34():
+        @pl.loop(0, 2)
+        def _(m13):
+            @pl.loop(0, 2)
+            def _(h):
+                q = 2 * m13 + h
+
+                @pl.loop(1, 16)
+                def _(k):
+                    a_copy(q, k).wait_recv()
+
+                s3[h] = dot3(matrix(3), halves(rr[q].reshape(512, 256)))
+
+            data = jnp.concatenate([s3[0], s3[1]], axis=1)
+            new = dot3(halves(data), matrix(4), True)
+            for h in range(2):
+                w[2 * m13 + h] = new[:, 256 * h : 256 * h + 256].reshape(4, 128, 256)
 
     def t_copy(i):
         return remote(acc.at[1 - core, i], twin.at[i], t_send.at[i], t_recv.at[i], sibling)
@@ -304,7 +334,7 @@
 
         @pl.loop(0, 4)
         def _(i):
-            data = s3[:, i].reshape(512, 256)
+            data = w[:, i].reshape(512, 256)
             new = dot3((bh[5, rows], bl[5, rows]), halves(data)).reshape(2, 8, 16, 256)
             if send:
                 acc[half, i] = new
@@ -338,62 +368,73 @@
             for d in range(2):
                 r_copy(k, d, steps(k, d)).wait_recv()
             final[k] = acc[core, :, k, y] + part[k, 0, steps(k, 0) - 1] + part[k, 1, steps(k, 1) - 1]
-        swap = remote(final.at[1 - xh], last, l_send, l_recv, across)
+        swap = remote(final.at[1 - xh_], last, l_send, l_recv, across)
         go(swap)
         swap.wait_recv()
-        out[...] = (final[xh] + last[...]).reshape(64, 256)
-
-    go(x_copy(0))
+        for i in range(4):
+            value = final[xh_, i] + last[i]
+            for n in range(4):
+                out[4 * i : 4 * i + 4, 256 * n : 256 * n + 256] = value[4 * n : 4 * n + 4]
+
+    multiply()
+    fragment(0)
+    fragment(1)
+    fragment(3)
+    pl.semaphore_wait(barrier, 19)
+    z_first(0)
     base_start(0)
-    z_step(0, 1)
+    fragment(2)
+    z_other(0)
+    y_step(0, 1)
+    fragment(4)
+    fragment(5)
     z_step(0, 2)
-    y_step(0, 1)
-    go(x_copy(1))
-    z_step(1, 1)
+    z_first(1)
+    y_step(0, 2)
+    split_stem()
     z_step(0, 3)
-    y_step(0, 2)
+    y_step(0, 3)
+    z_step(1, 2)
+    base_start(1)
+    z_step(0, 4)
+    y_step(0, 4)
+    z_step(1, 3)
     y_step(1, 1)
-    base_start(1)
-    z_step(1, 2)
-    z_step(0, 4)
-    y_step(0, 3)
-    y_step(1, 2)
-    z_step(1, 3)
+    y_step(0, 5)
     z_finish(0)
-    y_step(0, 4)
-    y_step(1, 3)
     z_step(1, 4)
+    y_step(2, 1)
     prepare_line(0)
     absorb0()
-    y_step(0, 5)
-    y_step(1, 4)
-    y_step(2, 1)
+    y_step(1, 2)
+    z_step(1, 5)
+    y_step(2, 2)
     y_finish(0)
     prepare_turned(0)
     absorb1()
-    y_step(1, 5)
-    y_step(2, 2)
-    y_step(3, 1)
-    y_finish(1)
-    prepare_ring(1)
-    absorb4()
+    y_step(1, 3)
     y_step(2, 3)
-    y_step(3, 2)
     z_finish(1)
     prepare_line(1)
     absorb2()
+    y_step(1, 4)
     y_step(2, 4)
+    y_step(3, 1)
+    y_step(1, 5)
+    y_step(2, 5)
+    y_step(3, 2)
+    y_finish(1)
+    prepare_ring(1)
     y_step(3, 3)
-    y_step(2, 5)
     y_finish(2)
     prepare_ring(2)
     y_step(3, 4)
     y_step(3, 5)
     y_finish(3)
     new = lax.broadcasted_iota(I32, (128, 128), 0)
-    old = reordered(new, (2, 3, 4, 0, 1, 5, 6))
+    old = reordered(new, (2, 3, 4, 5, 6, 0, 1))
     prepare_turned(3, one_hot(lax.broadcasted_iota(I32, (128, 128), 1), old))
-    absorb3()
+    absorb34()
     absorb5(1 - core, True)
     absorb5(core, False)
     reduce()
@@ -416,45 +457,43 @@
 
 
 def per_device(stem, left, right, slice_bits, leg_order):
-    smem, vmem = pl.BlockSpec(memory_space=pltpu.SMEM), pl.BlockSpec(memory_space=pltpu.VMEM)
-    shape = jax.ShapeDtypeStruct
-    fz, fy, sel = pl.pallas_call(
-        fragments,
-        out_shape=(shape((2, 32, 512), F32), shape((4, 8, 2, 8, 256), F32), shape((4, 8, 256), I32)),
-        in_specs=[smem, smem, vmem, vmem],
-        out_specs=(vmem, vmem, vmem),
-        compiler_params=pltpu.CompilerParams(vmem_limit_bytes=32 * 2**20),
-    )(leg_order, slice_bits, left, right)
+    smem, anywhere = pl.BlockSpec(memory_space=pltpu.SMEM), pl.BlockSpec(memory_space=pl.ANY)
     dma = pltpu.SemaphoreType.DMA
     result = pl.pallas_call(
         contract,
-        out_shape=shape((64, 256), F32),
-        in_specs=[vmem, vmem, vmem, vmem],
-        out_specs=vmem,
+        out_shape=jax.ShapeDtypeStruct((16, 1024), F32),
+        in_specs=[smem, smem, anywhere, anywhere, anywhere],
+        out_specs=pl.BlockSpec(memory_space=pltpu.VMEM),
         scratch_shapes=[
+            pltpu.VMEM((6, 2, 32, 512), F32),
+            pltpu.VMEM((512, 512), F32),
+            pltpu.VMEM((16, 32768), F32),
+            pltpu.VMEM((384, 512), F32),
+            pltpu.VMEM((4, 8, 2, 8, 256), F32),
+            pltpu.VMEM((1024, 512), BF16),
+            pltpu.VMEM((1024, 512), BF16),
             pltpu.VMEM((2, 16, 32, 512), F32),
             pltpu.VMEM((4, 8, 2, 16, 8, 256), F32),
             pltpu.VMEM((6, 512, 512), BF16),
             pltpu.VMEM((6, 512, 512), BF16),
             pltpu.VMEM((1024, 512), F32),
-            pltpu.VMEM((2, 4, 2, 128, 256), F32),
             pltpu.VMEM((4, 4, 128, 256), F32),
             pltpu.VMEM((4, 16, 32, 256), F32),
             pltpu.VMEM((4, 16, 32, 256), F32),
-            pltpu.VMEM((4, 4, 128, 256), F32),
+            pltpu.VMEM((2, 512, 256), F32),
             pltpu.VMEM((2, 4, 2, 8, 16, 256), F32),
             pltpu.VMEM((4, 2, 8, 16, 256), F32),
             pltpu.VMEM((2, 2, 4, 4, 16, 256), F32),
             pltpu.VMEM((2, 4, 16, 256), F32),
             pltpu.VMEM((4, 16, 256), F32),
-            dma((2, 2, 2, 4)), dma((2, 2, 2, 4)), dma((2,)), dma((2,)),
+            dma((3,)), dma((2, 2, 2, 4)), dma((2, 2, 2, 4)), dma((2, 8)), dma((2, 8)),
             dma((2, 16)), dma((2, 16)), dma((4, 2, 4)), dma((4, 2, 4)), dma((4, 8)), dma((4, 8)),
             dma((4, 16)), dma((4, 16)), dma((4,)), dma((4,)), dma((2, 2, 4)), dma((2, 2, 4)), dma, dma,
         ],
         compiler_params=pltpu.CompilerParams(
             collective_id=0, has_side_effects=True, vmem_limit_bytes=56 * 2**20
         ),
-    )(stem.reshape(1024, 512), fz, fy, sel)
+    )(leg_order, slice_bits, stem.reshape(16, 32768), left, right)
     return result.reshape(16, 1, 1024)
 
 

time: 155 us -> 135 us (0.87)
  Pallas kernels: 144 us -> 133 us
  local copies, waits for them, and re-layouts: 10.1 us -> 1.54 us
    pallas_call x2 -> x1, Pallas kernels: 144 us -> 133 us  [per_device(): pl.pallas_call(contract, out_shape=jax.ShapeDtypeStruct((16, 1024), F32),...]
    unnamed x14 -> x0, local copies, waits for them, and re-layouts: 5.76 us -> none
    reshape x1 -> x0, local copies, waits for them, and re-layouts: 2.77 us -> none  [per_device(): stem.reshape(1024, 512)]
where the time goes in v2:
time: 135 us
  Pallas kernels  133 us (99%)
  local copies, waits for them, and re-layouts  1.54 us (1%)
    pallas_call x1, Pallas kernels, per_device(): pl.pallas_call(contract, out_shape=jax.ShapeDtypeStruct((16, 1024), F32),...  133 us

profile of v2, /device:TPU:8, one launch (start us, length us, event | category | flops | bytes accessed | tf_op | source)
XLA Modules:
  0.0 134.7 jit_solution(15868886215592565681)
XLA Ops:
  0.0 133.1 %shard_map.55 = f32[16,1024]{1,0:T(8,128)} custom-call(s32[6,9]{1,0:T(8,128)} %order.1, s32[1,6]{1,0:T(1,128)} %bits.1, f32[16,32768]{1,0:T(8,128)} %bitcast.2, f32[6,2,32,512]{3,2,1,0:T(8,128)} %left_hbm.1, f32[512,512]{1,0:T(8,128)} %right_hbm.1), custom_call_target="tpu_custom_call" | custom-call | tf_op jit(solution)/shard_map/pallas_call | solution.py:462
  133.1 1.5 %copy.6 = f32[16,1,1024]{2,1,0:T(1,128)} copy(f32[16,1,1024]{2,0,1:T(8,128)} %bitcast.3) | data formatting | bytes 131072 | tf_op jit(solution)/shard_map/reshape | solution.py:497

commit v3 on v2

--- a/solution.py
+++ b/solution.py
@@ -9,8 +9,9 @@
 
 F32, BF16, I32 = jnp.float32, jnp.bfloat16, jnp.int32
 MESH = pl.DeviceIdType.MESH
-LINE = (0, 2)
-RING = (1, 3, 4, 5)
+LINE = (0,)
+RING = (1, 2, 3, 4, 5)
+GROUPS = ((0, 1), (1, 2), (3, 2))
 NATURAL9 = (0, 1, 2, 3, 4, 5, 6, 7, 8)
 COLUMNS = {1: (8, 2, 3, 4, 5, 6, 7, 0, 1), 5: (7, 8, 0, 1, 2, 3, 4, 5, 6)}
 ROWS = {1: (3, 4, 0, 1, 2), 5: (2, 1, 0, 3, 4)}
@@ -48,6 +49,7 @@
     order, bits, stem_hbm, left_hbm, right_hbm, out,
     left, right, stem, product, fy, xh, xl_, gz, gy, bh, bl, y0, w, tt, rr, s3, acc, twin, part, final, last,
     in_sem, z_send, z_recv, x_send, x_recv, base_send, base_recv, y_send, y_recv, d_send, d_recv,
+    e_send, e_recv, f_send,
     a_send, a_recv, t_send, t_recv, r_send, r_recv, l_send, l_recv,
 ):
     c, m = lax.axis_index("cuts"), lax.axis_index("mode")
@@ -58,6 +60,7 @@
     sibling = (c + 1 - 2 * core, m)
     across = (c + 2 - 4 * xh_, m)
     beside = (c, m + 8 - 16 * xl)
+    corner = (c + 2 - 4 * xh_, m + 8 - 16 * xl)
 
     def peer(k):
         return lax.rem(m + k, 16)
@@ -68,7 +71,7 @@
     def _(k):
         pl.semaphore_signal(barrier, inc=1, device_id=(c, peer(k)), device_id_type=MESH)
 
-    for target in (*y_next, sibling, across):
+    for target in (*y_next, sibling, across, corner):
         pl.semaphore_signal(barrier, inc=1, device_id=target, device_id_type=MESH)
 
     loads = [
@@ -78,16 +81,16 @@
     for load in loads:
         load.start()
 
-    started = []
-
     def remote(src, dst, send, recv, target):
         return pltpu.make_async_remote_copy(
             src_ref=src, dst_ref=dst, send_sem=send, recv_sem=recv, device_id=target, device_id_type=MESH
         )
 
+    def settle(ref, sem):
+        pltpu.make_async_copy(ref, ref, sem).wait()
+
     def go(copy):
         copy.start()
-        started.append(copy)
 
     def multiply():
         loads[0].wait()
@@ -117,7 +120,7 @@
         value = pieces[0] + pieces[1] + pieces[2]
         if t in LINE:
             wide = jnp.full((32, 512), bits[0, t], I32)
-            gz[LINE.index(t), m] = jnp.where(wide == 1, value[32:], value[:32])
+            gz[m] = jnp.where(wide == 1, value[32:], value[:32])
         else:
             k = RING.index(t)
             for s in range(8):
@@ -139,105 +142,107 @@
                     rows = pl.ds(pl.multiple_of(256 * (2 * m4 + m5) + 16 * i, 16), 16)
                     xh[rows], xl_[rows] = halves(jnp.concatenate(tiles, axis=0))
 
-    def x_copy(k, n):
-        if n == 0:
-            owner = z
-        elif n == 7:
-            owner = lax.rem(z + 4, 8)
-        else:
-            owner = lax.rem(z + 8 - (1 - 2 * ((n - 1) % 2)) * ((n + 1) // 2), 8)
-        piece = gz.at[k, xl * 8 + owner]
-        return remote(piece, piece, x_send.at[k, n], x_recv.at[k, n], beside)
-
-    def z_copy(k, cls, d, s):
+    def x_copy():
+        return remote(gz.at[m], gz.at[m], x_send, x_recv, beside)
+
+    def z_copy(cls, d, s):
         owner = lax.rem(z + 8 - (1 - 2 * d) * (s - 1), 8)
         row = (xl * 8 if cls == 0 else (1 - xl) * 8) + owner
-        piece = gz.at[k, row]
+        piece = gz.at[row]
         if s == 4:
-            piece = gz.at[k, row, pl.ds(16 * d, 16)]
-        return remote(piece, piece, z_send.at[k, cls, d, s - 1], z_recv.at[k, cls, d, s - 1], z_next[d])
-
-    def z_first(k):
-        go(x_copy(k, 0))
+            piece = gz.at[row, pl.ds(16 * d, 16)]
+        return remote(piece, piece, z_send, z_recv.at[cls, d, s - 1], z_next[d])
+
+    def z_first():
+        go(x_copy())
         for d in range(2):
-            go(z_copy(k, 0, d, 1))
-
-    def z_other(k):
-        x_copy(k, 0).wait_recv()
+            go(z_copy(0, d, 1))
+
+    def z_other():
+        x_copy().wait_recv()
         for d in range(2):
-            go(z_copy(k, 1, d, 1))
-
-    def z_step(k, s):
-        for cls in range(2 if k == 0 else 1):
+            go(z_copy(1, d, 1))
+
+    def z_step(s):
+        for cls in range(2):
             for d in range(2):
-                z_copy(k, cls, d, s - 1).wait_recv()
+                z_copy(cls, d, s - 1).wait_recv()
                 if s < 5:
-                    go(z_copy(k, cls, d, s))
-                    if k == 1:
-                        go(x_copy(k, 2 * (s - 1) - 1 + d))
-        if k == 1 and s == 5:
-            go(x_copy(k, 7))
-
-    def z_finish(k):
-        if k == 0:
-            z_step(0, 5)
-        else:
-            for n in range(8):
-                x_copy(k, n).wait_recv()
+                    go(z_copy(cls, d, s))
 
     def base_copy(g, k):
-        pair = pl.ds(2 * g, 2)
+        pair = pl.ds(*GROUPS[g])
         return remote(
             fy.at[pair, y, core], gy.at[pair, y, core, m],
-            base_send.at[g, k], base_recv.at[g, k], (c, peer(k)),
+            base_send, base_recv.at[g], (c, xl * 8 + lax.rem(z + k, 8)),
         )
 
     def base_start(g):
-        @pl.loop(1, 16)
+        @pl.loop(1, 8)
         def _(k):
             base_copy(g, k).start()
 
     def base_wait(g):
-        @pl.loop(1, 16)
-        def _(k):
-            base_copy(g, k).wait_recv()
+        settle(gy.at[pl.ds(*GROUPS[g]), y, core, pl.ds(0, 7)], base_recv.at[g])
 
     def y_copy(t, d, s):
         owner = lax.rem(y + 8 - (1 - 2 * d) * (s - 1), 8)
-        piece = gy.at[t, owner, core]
+        piece = gy.at[t, owner, core, pl.ds(8 * xl, 8)]
         if s == 4:
-            piece = gy.at[t, owner, core, pl.ds(8 * d, 8)]
-        return remote(piece, piece, y_send.at[t, d, s - 1], y_recv.at[t, d, s - 1], y_next[d])
+            piece = gy.at[t, owner, core, pl.ds(8 * xl + 4 * d, 4)]
+        return remote(piece, piece, y_send, y_recv.at[t, d, s - 1], y_next[d])
+
+    def slot(n):
+        if n == 0:
+            return y
+        if n == 7:
+            return lax.rem(y + 4, 8)
+        return lax.rem(y + 8 - (1 - 2 * ((n - 1) % 2)) * ((n + 1) // 2), 8)
 
     def d_copy(t, n):
-        if n == 0:
-            slot = y
-        elif n == 7:
-            slot = lax.rem(y + 4, 8)
-        else:
-            slot = lax.rem(y + 8 - (1 - 2 * ((n - 1) % 2)) * ((n + 1) // 2), 8)
-        piece = gy.at[t, slot, core]
-        return remote(piece, piece, d_send.at[t, n], d_recv.at[t, n], sibling)
+        piece = gy.at[t, slot(n), core, pl.ds(8 * xl, 8)]
+        return remote(piece, piece, d_send, d_recv.at[t], sibling)
+
+    def e_copy(t, n, e):
+        piece = gy.at[t, slot(n), core, pl.ds(8 * xl + 4 * e, 4)]
+        return remote(piece, piece, e_send, e_recv.at[t, n], corner if e else beside)
+
+    def f_copy(t, n):
+        piece = gy.at[t, slot(n), core, pl.ds(8 - 8 * xl, 8)]
+        return remote(piece, piece, f_send, d_recv.at[t], sibling)
+
+    def share(t, n):
+        for e in range(2):
+            go(e_copy(t, n, e))
+        go(d_copy(t, n))
+
+    def relay(t, n):
+        settle(gy.at[t, slot(n), core, pl.ds(8 - 8 * xl, 8)], e_recv.at[t, n])
+        go(f_copy(t, n))
 
     def y_step(t, s):
         if s == 1:
-            if t % 2 == 0:
-                base_wait(t // 2)
+            for g, (first, _) in enumerate(GROUPS):
+                if t == first:
+                    base_wait(g)
             for d in range(2):
                 go(y_copy(t, d, 1))
-            go(d_copy(t, 0))
+            share(t, 0)
             return
         for d in range(2):
             y_copy(t, d, s - 1).wait_recv()
             if s < 5:
                 go(y_copy(t, d, s))
-                go(d_copy(t, 2 * (s - 1) - 1 + d))
-        if s == 5:
-            go(d_copy(t, 7))
+        if s < 5:
+            for d in range(2):
+                share(t, 2 * s - 3 + d)
+        else:
+            share(t, 7)
+        for n in (0,) if s == 2 else (2 * s - 5, 2 * s - 4):
+            relay(t, n)
 
     def y_finish(t):
-        for n in range(8):
-            d_copy(t, n).wait_recv()
+        settle(gy.at[t, :, 1 - core], d_recv.at[t])
 
     def prepare_line(k):
         b = LINE[k]
@@ -245,7 +250,7 @@
         @pl.loop(0, 4)
         def _(i):
             rows = pl.ds(pl.multiple_of(128 * i, 128), 128)
-            bh[b, rows], bl[b, rows] = halves(gz[k, pl.ds(4 * i, 4)].reshape(128, 512))
+            bh[b, rows], bl[b, rows] = halves(gz[pl.ds(4 * i, 4)].reshape(128, 512))
 
     def prepare_ring(t):
         b = RING[t]
@@ -294,7 +299,7 @@
 
     def a_copy(q, k):
         return remote(
-            tt.at[q, peer(k)], rr.at[q, m], a_send.at[q, k], a_recv.at[q, k], (c, peer(k))
+            tt.at[q, peer(k)], rr.at[q, m], a_send, a_recv.at[q], (c, peer(k))
         )
 
     def absorb2():
@@ -315,10 +320,7 @@
             def _(h):
                 q = 2 * m13 + h
 
-                @pl.loop(1, 16)
-                def _(k):
-                    a_copy(q, k).wait_recv()
-
+                settle(rr.at[q, pl.ds(0, 15)], a_recv.at[q])
                 s3[h] = dot3(matrix(3), halves(rr[q].reshape(512, 256)))
 
             data = jnp.concatenate([s3[0], s3[1]], axis=1)
@@ -327,12 +329,12 @@
                 w[2 * m13 + h] = new[:, 256 * h : 256 * h + 256].reshape(4, 128, 256)
 
     def t_copy(i):
-        return remote(acc.at[1 - core, i], twin.at[i], t_send.at[i], t_recv.at[i], sibling)
-
-    def absorb5(half, send):
+        return remote(acc.at[1 - core, i], twin.at[i], t_send, t_recv.at[i], sibling)
+
+    def absorb5(half, low, send):
         rows = pl.ds(pl.multiple_of(256 * half, 256), 256)
 
-        @pl.loop(0, 4)
+        @pl.loop(low, low + 2)
         def _(i):
             data = w[:, i].reshape(512, 256)
             new = dot3((bh[5, rows], bl[5, rows]), halves(data)).reshape(2, 8, 16, 256)
@@ -343,117 +345,134 @@
                 t_copy(i).wait_recv()
                 acc[half, i] = new + twin[i]
 
+    CHAINS = ((0, 0), (1, 1), (0, 1), (1, 0))
+
     def steps(k, d):
         return 4 if k == d else 3
 
-    def r_copy(k, d, s):
-        n = steps(k, d)
-        dest = lax.rem(y + 8 + (1 - 2 * d) * (n - s + 1), 8)
-        src = acc.at[core, :, k, dest] if s == 1 else part.at[k, d, s - 2]
-        return remote(src, part.at[k, d, s - 1], r_send.at[k, d, s - 1], r_recv.at[k, d, s - 1], y_next[d])
-
-    def reduce():
-        order = [(k, d) for d in range(2) for k in range(2)]
-        for k, d in order:
-            go(r_copy(k, d, 1))
-        for s in range(2, 5):
-            for k, d in order:
-                n = steps(k, d)
-                if s <= n:
-                    dest = lax.rem(y + 8 + (1 - 2 * d) * (n - s + 1), 8)
-                    r_copy(k, d, s - 1).wait_recv()
-                    part[k, d, s - 2] = part[k, d, s - 2] + acc[core, :, k, dest]
-                    go(r_copy(k, d, s))
+    def r_dest(k, d, s):
+        return lax.rem(y + 8 + (1 - 2 * d) * (steps(k, d) - s + 1), 8)
+
+    def r_copy(p, k, d, s):
+        src = acc.at[core, pl.ds(2 * p, 2), k, r_dest(k, d, s)] if s == 1 else part.at[p, k, d, s - 2]
+        return remote(
+            src, part.at[p, k, d, s - 1], r_send, r_recv.at[p, k, d, s - 1], y_next[d]
+        )
+
+    def r_step(p, s):
+        for k, d in CHAINS:
+            if s <= steps(k, d):
+                if s > 1:
+                    r_copy(p, k, d, s - 1).wait_recv()
+                    part[p, k, d, s - 2] += acc[core, 2 * p : 2 * p + 2, k, r_dest(k, d, s)]
+                go(r_copy(p, k, d, s))
+
+    def l_copy(p):
+        return remote(final.at[p, 1 - xh_], last.at[p], l_send, l_recv.at[p], across)
+
+    def r_finish(p):
         for k in range(2):
             for d in range(2):
-                r_copy(k, d, steps(k, d)).wait_recv()
-            final[k] = acc[core, :, k, y] + part[k, 0, steps(k, 0) - 1] + part[k, 1, steps(k, 1) - 1]
-        swap = remote(final.at[1 - xh_], last, l_send, l_recv, across)
-        go(swap)
-        swap.wait_recv()
-        for i in range(4):
-            value = final[xh_, i] + last[i]
+                r_copy(p, k, d, steps(k, d)).wait_recv()
+            total = part[p, k, 0, steps(k, 0) - 1] + part[p, k, 1, steps(k, 1) - 1]
+            final[p, k] = acc[core, 2 * p : 2 * p + 2, k, y] + total
+        go(l_copy(p))
+
+    def write(p):
+        l_copy(p).wait_recv()
+        for i in range(2):
+            value = final[p, xh_, i] + last[p, i]
+            rows = slice(8 * p + 4 * i, 8 * p + 4 * i + 4)
             for n in range(4):
-                out[4 * i : 4 * i + 4, 256 * n : 256 * n + 256] = value[4 * n : 4 * n + 4]
+                out[rows, 256 * n : 256 * n + 256] = value[4 * n : 4 * n + 4]
 
     multiply()
     fragment(0)
     fragment(1)
-    fragment(3)
-    pl.semaphore_wait(barrier, 19)
-    z_first(0)
+    pl.semaphore_wait(barrier, 20)
+    z_first()
     base_start(0)
     fragment(2)
-    z_other(0)
-    y_step(0, 1)
+    fragment(3)
+    base_start(1)
     fragment(4)
     fragment(5)
-    z_step(0, 2)
-    z_first(1)
+    z_other()
+    y_step(0, 1)
+    z_step(2)
     y_step(0, 2)
+    y_step(1, 1)
+    z_step(3)
+    y_step(0, 3)
+    y_step(1, 2)
     split_stem()
-    z_step(0, 3)
-    y_step(0, 3)
-    z_step(1, 2)
-    base_start(1)
-    z_step(0, 4)
     y_step(0, 4)
-    z_step(1, 3)
-    y_step(1, 1)
+    z_step(4)
+    base_start(2)
+    y_step(1, 3)
     y_step(0, 5)
-    z_finish(0)
-    z_step(1, 4)
-    y_step(2, 1)
+    z_step(5)
+    y_step(1, 4)
+    relay(0, 7)
     prepare_line(0)
     absorb0()
-    y_step(1, 2)
-    z_step(1, 5)
-    y_step(2, 2)
+    y_step(1, 5)
     y_finish(0)
     prepare_turned(0)
+    relay(1, 7)
     absorb1()
-    y_step(1, 3)
-    y_step(2, 3)
-    z_finish(1)
-    prepare_line(1)
-    absorb2()
-    y_step(1, 4)
-    y_step(2, 4)
-    y_step(3, 1)
-    y_step(1, 5)
-    y_step(2, 5)
-    y_step(3, 2)
     y_finish(1)
     prepare_ring(1)
+    absorb2()
+    y_step(2, 1)
+    y_step(3, 1)
+    y_step(2, 2)
+    y_step(3, 2)
+    y_step(4, 1)
+    y_step(2, 3)
     y_step(3, 3)
+    y_step(4, 2)
+    y_step(2, 4)
+    y_step(3, 4)
+    y_step(4, 3)
+    y_step(2, 5)
+    y_step(3, 5)
+    relay(2, 7)
+    relay(3, 7)
+    y_step(4, 4)
     y_finish(2)
     prepare_ring(2)
-    y_step(3, 4)
-    y_step(3, 5)
+    y_step(4, 5)
     y_finish(3)
+    prepare_ring(3)
+    relay(4, 7)
+    y_finish(4)
     new = lax.broadcasted_iota(I32, (128, 128), 0)
     old = reordered(new, (2, 3, 4, 5, 6, 0, 1))
-    prepare_turned(3, one_hot(lax.broadcasted_iota(I32, (128, 128), 1), old))
+    prepare_turned(4, one_hot(lax.broadcasted_iota(I32, (128, 128), 1), old))
     absorb34()
-    absorb5(1 - core, True)
-    absorb5(core, False)
-    reduce()
-
-    for copy in started:
-        copy.wait_send()
-
-    @pl.loop(1, 16)
-    def _(k):
-        for g in range(2):
-            base_copy(g, k).wait_send()
-
-    @pl.loop(0, 4)
-    def _(q):
-        t_copy(q).wait_send()
-
-        @pl.loop(1, 16)
-        def _(k):
-            a_copy(q, k).wait_send()
+    for p in range(2):
+        absorb5(1 - core, 2 * p, True)
+        absorb5(core, 2 * p, False)
+        r_step(p, 1)
+    for s in range(2, 5):
+        for p in range(2):
+            r_step(p, s)
+    for p in range(2):
+        r_finish(p)
+    for p in range(2):
+        write(p)
+
+    x_copy().wait_send()
+    settle(gz.at[pl.ds(0, 14)], z_send)
+    settle(fy.at[:, pl.ds(0, 7), 0], base_send)
+    settle(gy.at[:, pl.ds(0, 7), 0, pl.ds(0, 8)], y_send)
+    for sem in (d_send, e_send, f_send):
+        settle(gy.at[:, :, 0, pl.ds(0, 8)], sem)
+    settle(tt.at[:, pl.ds(0, 15)], a_send)
+    settle(acc.at[0], t_send)
+    settle(tt.at[:, pl.ds(0, 7)], r_send)
+    settle(last, l_send)
 
 
 def per_device(stem, left, right, slice_bits, leg_order):
@@ -469,11 +488,11 @@
             pltpu.VMEM((512, 512), F32),
             pltpu.VMEM((16, 32768), F32),
             pltpu.VMEM((384, 512), F32),
-            pltpu.VMEM((4, 8, 2, 8, 256), F32),
+            pltpu.VMEM((5, 8, 2, 8, 256), F32),
             pltpu.VMEM((1024, 512), BF16),
             pltpu.VMEM((1024, 512), BF16),
-            pltpu.VMEM((2, 16, 32, 512), F32),
-            pltpu.VMEM((4, 8, 2, 16, 8, 256), F32),
+            pltpu.VMEM((16, 32, 512), F32),
+            pltpu.VMEM((5, 8, 2, 16, 8, 256), F32),
             pltpu.VMEM((6, 512, 512), BF16),
             pltpu.VMEM((6, 512, 512), BF16),
             pltpu.VMEM((1024, 512), F32),
@@ -483,12 +502,14 @@
             pltpu.VMEM((2, 512, 256), F32),
             pltpu.VMEM((2, 4, 2, 8, 16, 256), F32),
             pltpu.VMEM((4, 2, 8, 16, 256), F32),
-            pltpu.VMEM((2, 2, 4, 4, 16, 256), F32),
-            pltpu.VMEM((2, 4, 16, 256), F32),
-            pltpu.VMEM((4, 16, 256), F32),
-            dma((3,)), dma((2, 2, 2, 4)), dma((2, 2, 2, 4)), dma((2, 8)), dma((2, 8)),
-            dma((2, 16)), dma((2, 16)), dma((4, 2, 4)), dma((4, 2, 4)), dma((4, 8)), dma((4, 8)),
-            dma((4, 16)), dma((4, 16)), dma((4,)), dma((4,)), dma((2, 2, 4)), dma((2, 2, 4)), dma, dma,
+            pltpu.VMEM((2, 2, 2, 4, 2, 16, 256), F32),
+            pltpu.VMEM((2, 2, 2, 16, 256), F32),
+            pltpu.VMEM((2, 2, 16, 256), F32),
+            dma((3,)), dma, dma((2, 2, 4)), dma, dma,
+            dma, dma((3,)), dma, dma((5, 2, 4)), dma, dma((5,)),
+            dma, dma((5, 8)), dma,
+            dma, dma((4,)), dma, dma((4,)),
+            dma, dma((2, 2, 2, 4)), dma, dma((2,)),
         ],
         compiler_params=pltpu.CompilerParams(
             collective_id=0, has_side_effects=True, vmem_limit_bytes=56 * 2**20

time: 135 us -> 122 us (0.904)
  Pallas kernels: 133 us -> 120 us
    pallas_call x1, Pallas kernels: 133 us -> 120 us  [per_device(): pl.pallas_call(contract, out_shape=jax.ShapeDtypeStruct((16, 1024), F32),...]
where the time goes in v3:
time: 122 us
  Pallas kernels  120 us (98%)
  local copies, waits for them, and re-layouts  1.54 us (1%)
    pallas_call x1, Pallas kernels, per_device(): pl.pallas_call(contract, out_shape=jax.ShapeDtypeStruct((16, 1024), F32),...  120 us

profile of v3, /device:TPU:8, one launch (start us, length us, event | category | flops | bytes accessed | tf_op | source)
XLA Modules:
  0.0 121.8 jit_solution(18166922698505029878)
XLA Ops:
  0.0 120.3 %shard_map.55 = f32[16,1024]{1,0:T(8,128)} custom-call(s32[6,9]{1,0:T(8,128)} %order.1, s32[1,6]{1,0:T(1,128)} %bits.1, f32[16,32768]{1,0:T(8,128)} %bitcast.2, f32[6,2,32,512]{3,2,1,0:T(8,128)} %left_hbm.1, f32[512,512]{1,0:T(8,128)} %right_hbm.1), custom_call_target="tpu_custom_call" | custom-call | tf_op jit(solution)/shard_map/pallas_call | solution.py:481
  120.3 1.5 %copy.6 = f32[16,1,1024]{2,1,0:T(1,128)} copy(f32[16,1,1024]{2,0,1:T(8,128)} %bitcast.3) | data formatting | bytes 131072 | tf_op jit(solution)/shard_map/reshape | solution.py:518

commit v4 on v3

--- a/solution.py
+++ b/solution.py
@@ -46,10 +46,10 @@
 
 
 def contract(
-    order, bits, stem_hbm, left_hbm, right_hbm, out,
-    left, right, stem, product, fy, xh, xl_, gz, gy, bh, bl, y0, w, tt, rr, s3, acc, twin, part, final, last,
+    order_hbm, bits_hbm, stem_hbm, left_hbm, right_hbm, out,
+    order, bits, left, right, stem, product, fy, xh, xl_, gz, gy, bh, bl, y0, w, tt, rr, s3, acc, twin, part, final, last,
     in_sem, z_send, z_recv, x_send, x_recv, base_send, base_recv, y_send, y_recv, d_send, d_recv,
-    e_send, e_recv, f_send,
+    e_send, e_recv, f_send, f_recv,
     a_send, a_recv, t_send, t_recv, r_send, r_recv, l_send, l_recv,
 ):
     c, m = lax.axis_index("cuts"), lax.axis_index("mode")
@@ -76,7 +76,7 @@
 
     loads = [
         pltpu.make_async_copy(src, dst, in_sem.at[n])
-        for n, (src, dst) in enumerate(((right_hbm, right), (left_hbm, left), (stem_hbm, stem)))
+        for n, (src, dst) in enumerate(((right_hbm, right), (left_hbm, left), (stem_hbm, stem), (order_hbm, order), (bits_hbm, bits)))
     ]
     for load in loads:
         load.start()
@@ -95,6 +95,8 @@
     def multiply():
         loads[0].wait()
         loads[1].wait()
+        loads[3].wait()
+        loads[4].wait()
         product[...] = dot3(halves(left[...].reshape(384, 512)), halves(right[...]))
 
     def fragment(t):
@@ -209,7 +211,7 @@
 
     def f_copy(t, n):
         piece = gy.at[t, slot(n), core, pl.ds(8 - 8 * xl, 8)]
-        return remote(piece, piece, f_send, d_recv.at[t], sibling)
+        return remote(piece, piece, f_send, f_recv.at[t], sibling)
 
     def share(t, n):
         for e in range(2):
@@ -241,8 +243,15 @@
         for n in (0,) if s == 2 else (2 * s - 5, 2 * s - 4):
             relay(t, n)
 
+    def own_finish(t):
+        settle(gy.at[t, :, 1 - core, pl.ds(8 * xl, 8)], d_recv.at[t])
+
+    def other_finish(t):
+        settle(gy.at[t, :, 1 - core, pl.ds(8 - 8 * xl, 8)], f_recv.at[t])
+
     def y_finish(t):
-        settle(gy.at[t, :, 1 - core], d_recv.at[t])
+        own_finish(t)
+        other_finish(t)
 
     def prepare_line(k):
         b = LINE[k]
@@ -252,11 +261,11 @@
             rows = pl.ds(pl.multiple_of(128 * i, 128), 128)
             bh[b, rows], bl[b, rows] = halves(gz[pl.ds(4 * i, 4)].reshape(128, 512))
 
-    def prepare_ring(t):
+    def prepare_ring(t, low=0, count=16):
         b = RING[t]
         one = jnp.full((8, 256), bits[0, b], I32) == 1
 
-        @pl.loop(0, 16)
+        @pl.loop(low, low + count)
         def _(i):
             rows = pl.ds(pl.multiple_of(32 * i, 32), 32)
             for h in range(2):
@@ -297,21 +306,22 @@
             data = jnp.concatenate([y0[rows, :256], y0[rows, 256:]], axis=0)
             w[:, i] = dot3(matrix(1), halves(data)).reshape(4, 128, 256)
 
-    def a_copy(q, k):
-        return remote(
-            tt.at[q, peer(k)], rr.at[q, m], a_send, a_recv.at[q], (c, peer(k))
-        )
-
-    def absorb2():
+    def a_copy(q, target):
+        return remote(tt.at[q, target], rr.at[q, m], a_send, a_recv.at[q], (c, target))
+
+    def absorb2(cls, own):
+        rows = pl.ds(pl.multiple_of(256 * cls, 256), 256)
+
         @pl.loop(0, 4)
         def _(q):
-            new = dot3(matrix(2), halves(w[q].reshape(512, 256)))
-            tt[q] = new.reshape(16, 32, 256)
-            rr[q, m] = tt[q, m]
-
-            @pl.loop(1, 16)
+            new = dot3((bh[2, rows], bl[2, rows]), halves(w[q].reshape(512, 256)))
+            tt[q, pl.ds(8 * cls, 8)] = new.reshape(8, 32, 256)
+            if own:
+                rr[q, m] = tt[q, m]
+
+            @pl.loop(1 if own else 0, 8)
             def _(k):
-                a_copy(q, k).start()
+                a_copy(q, 8 * cls + lax.rem(z + k, 8)).start()
 
     def absorb34():
         @pl.loop(0, 2)
@@ -419,11 +429,14 @@
     y_step(1, 5)
     y_finish(0)
     prepare_turned(0)
+    absorb1()
+    own_finish(1)
+    prepare_ring(1, 8 * xl, 8)
+    absorb2(xl, True)
     relay(1, 7)
-    absorb1()
-    y_finish(1)
-    prepare_ring(1)
-    absorb2()
+    other_finish(1)
+    prepare_ring(1, 8 - 8 * xl, 8)
+    absorb2(1 - xl, False)
     y_step(2, 1)
     y_step(3, 1)
     y_step(2, 2)
@@ -481,9 +494,11 @@
     result = pl.pallas_call(
         contract,
         out_shape=jax.ShapeDtypeStruct((16, 1024), F32),
-        in_specs=[smem, smem, anywhere, anywhere, anywhere],
+        in_specs=[anywhere, anywhere, anywhere, anywhere, anywhere],
         out_specs=pl.BlockSpec(memory_space=pltpu.VMEM),
         scratch_shapes=[
+            pltpu.SMEM((6, 9), I32),
+            pltpu.SMEM((1, 6), I32),
             pltpu.VMEM((6, 2, 32, 512), F32),
             pltpu.VMEM((512, 512), F32),
             pltpu.VMEM((16, 32768), F32),
@@ -505,9 +520,9 @@
             pltpu.VMEM((2, 2, 2, 4, 2, 16, 256), F32),
             pltpu.VMEM((2, 2, 2, 16, 256), F32),
             pltpu.VMEM((2, 2, 16, 256), F32),
-            dma((3,)), dma, dma((2, 2, 4)), dma, dma,
+            dma((5,)), dma, dma((2, 2, 4)), dma, dma,
             dma, dma((3,)), dma, dma((5, 2, 4)), dma, dma((5,)),
-            dma, dma((5, 8)), dma,
+            dma, dma((5, 8)), dma, dma((5,)),
             dma, dma((4,)), dma, dma((4,)),
             dma, dma((2, 2, 2, 4)), dma, dma((2,)),
         ],

time: 122 us -> 120 us (0.984)
  the two profiles are of different devices: /device:TPU:8 before, /device:TPU:128 now
where the time goes in v4:
time: 120 us
  Pallas kernels  118 us (98%)
  local copies, waits for them, and re-layouts  1.54 us (1%)
    pallas_call x1, Pallas kernels, per_device(): pl.pallas_call(contract, out_shape=jax.ShapeDtypeStruct((16, 1024), F32),...  118 us

profile of v4, /device:TPU:128, one launch (start us, length us, event | category | flops | bytes accessed | tf_op | source)
XLA Modules:
  0.0 120.0 jit_solution(10345732775408858513)
XLA Ops:
  0.0 118.5 %shard_map.55 = f32[16,1024]{1,0:T(8,128)} custom-call(s32[6,9]{1,0:T(8,128)} %order_hbm.1, s32[1,6]{1,0:T(1,128)} %bits_hbm.1, f32[16,32768]{1,0:T(8,128)} %bitcast.2, f32[6,2,32,512]{3,2,1,0:T(8,128)} %left_hbm.1, f32[512,512]{1,0:T(8,128)} %right_hbm.1), custom_call_target="tpu_custom_call" | custom-call | tf_op jit(solution)/shard_map/pallas_call | solution.py:494
  118.5 1.5 %copy.6 = f32[16,1,1024]{2,1,0:T(1,128)} copy(f32[16,1,1024]{2,0,1:T(8,128)} %bitcast.3) | data formatting | bytes 131072 | tf_op jit(solution)/shard_map/reshape | solution.py:533

commit v5 on v4

--- a/solution.py
+++ b/solution.py
@@ -423,8 +423,8 @@
     y_step(0, 5)
     z_step(5)
     y_step(1, 4)
+    prepare_line(0)
     relay(0, 7)
-    prepare_line(0)
     absorb0()
     y_step(1, 5)
     y_finish(0)

time: 120 us -> 120 us (level)
  no operation moved by 1% of the time
where the time goes in v5:
time: 120 us
  Pallas kernels  118 us (98%)
  local copies, waits for them, and re-layouts  1.54 us (1%)
    pallas_call x1, Pallas kernels, per_device(): pl.pallas_call(contract, out_shape=jax.ShapeDtypeStruct((16, 1024), F32),...  118 us

profile of v5, /device:TPU:128, one launch (start us, length us, event | category | flops | bytes accessed | tf_op | source)
XLA Modules:
  0.0 119.7 jit_solution(11545299096583884167)
XLA Ops:
  0.0 118.2 %shard_map.55 = f32[16,1024]{1,0:T(8,128)} custom-call(s32[6,9]{1,0:T(8,128)} %order_hbm.1, s32[1,6]{1,0:T(1,128)} %bits_hbm.1, f32[16,32768]{1,0:T(8,128)} %bitcast.2, f32[6,2,32,512]{3,2,1,0:T(8,128)} %left_hbm.1, f32[512,512]{1,0:T(8,128)} %right_hbm.1), custom_call_target="tpu_custom_call" | custom-call | tf_op jit(solution)/shard_map/pallas_call | solution.py:494
  118.2 1.5 %copy.6 = f32[16,1,1024]{2,1,0:T(1,128)} copy(f32[16,1,1024]{2,0,1:T(8,128)} %bitcast.3) | data formatting | bytes 131072 | tf_op jit(solution)/shard_map/reshape | solution.py:533
